TPU v7x, 32 devices: a whole 2x2x4 slice. The times are simulated.
32 devices in a mesh: space: 8 (over z, y), tm: 4 (over x, core).
Axes of the slice: x: 2, y: 2, z: 4, core: 2. Of those that a mesh axis runs over, the one named last changes fastest.
Arguments:
- pw_field: float32 [96, 128, 36864], P('space', 'tm'), may hold values from -6 to 6
- cell_area: float32 [16, 36864], replicated, may hold values from 0.5 to 1.5
- tile_ids: int32 [96], replicated, may hold values from 0 to 95, as said below
- edge_table: int32 [3, 96, 4], replicated, may hold values from 0 to 95, as said below
Outputs:
- gram: float32 [128, 128], P('tm')
Inputs may be any that keep to these rules, and one draw needn't show every extreme that they name: A permutation: slot s holds the tile of face tile_ids[s] // 16, row (tile_ids[s] // 4) mod 4, column tile_ids[s] mod 4 of the face. `edge_table`: the cube's gluing for the slots of tile_ids: the neighbour slot and edge across each edge, and 1 where the two edges run in opposite directions; flags and edges lie in 0 to 1 and 0 to 3.
All inputs are finite; a program needn't handle non-finite values.
Results may differ from a plain program's by a relative error of at most 0.000051.
Values sent between devices are 32-bit elements; how exact they have to be, the bound alone decides.
A program may use at most 704 MiB of HBM per device.

v0:
```python
import jax
import jax.numpy as jnp
from jax import lax
from jax.sharding import PartitionSpec as P

STRIDE = 4
STEPS = 4
TILE = 192


def coefficient(step_idx):
    return 0.12 + 0.1 * step_idx / max(STEPS - 1, 1)


def edge_strips(weighted):
    return jnp.stack(
        [
            weighted[:, :, :TILE],
            weighted[:, :, -TILE:],
            weighted[:, :, 0::TILE],
            weighted[:, :, TILE - 1 :: TILE],
        ],
        axis=1,
    )


def pick_halo(all_strips, near_slot, near_edge, near_flip):
    snap_count = all_strips.shape[2]
    edge_width = all_strips.shape[3]
    flat_strips = all_strips.reshape(-1, snap_count, edge_width)
    position = (near_slot * 4 + near_edge).reshape(-1)
    chosen = jnp.take(flat_strips, position, axis=0).reshape(
        near_slot.shape[0], 4, snap_count, edge_width
    )
    return jnp.where((near_flip == 1)[:, :, None, None], chosen[..., ::-1], chosen)


def smooth_step(values, weighted, tile_area, halo_rows, factor):
    column = jnp.arange(TILE * TILE, dtype=jnp.int32) % TILE
    upper_nb = jnp.concatenate([halo_rows[:, 0], weighted[:, :, :-TILE]], axis=2)
    lower_nb = jnp.concatenate([weighted[:, :, TILE:], halo_rows[:, 1]], axis=2)
    left_shift = jnp.concatenate([weighted[:, :, :1], weighted[:, :, :-1]], axis=2)
    right_shift = jnp.concatenate([weighted[:, :, 1:], weighted[:, :, -1:]], axis=2)
    left_nb = jnp.where(column == 0, jnp.repeat(halo_rows[:, 2], TILE, axis=2), left_shift)
    right_nb = jnp.where(column == TILE - 1, jnp.repeat(halo_rows[:, 3], TILE, axis=2), right_shift)
    return (
        values
        + factor * (upper_nb + lower_nb + left_nb + right_nb - 4.0 * weighted) / tile_area[:, None]
    )


def subsample(values):
    shaped = values.reshape(values.shape[0], values.shape[1], TILE, TILE)[
        :, :, 1::STRIDE, 1::STRIDE
    ]
    return shaped.reshape(values.shape[0], values.shape[1], -1)


def body(pw_field, cell_area, tile_ids, edge_table):
    per_dev = pw_field.shape[0]
    snap_count = pw_field.shape[1]
    offset = lax.axis_index("space") * per_dev
    own_ids = lax.dynamic_slice_in_dim(tile_ids, offset, per_dev, 0)
    own_table = lax.dynamic_slice_in_dim(edge_table, offset, per_dev, 1)
    tile_area = jnp.take(cell_area, own_ids % cell_area.shape[0], axis=0)
    values = pw_field
    for step_idx in range(STEPS):
        weighted = tile_area[:, None] * values
        gathered = lax.all_gather(edge_strips(weighted), "space", axis=0, tiled=True)
        halo_rows = pick_halo(gathered, own_table[0], own_table[1], own_table[2])
        values = smooth_step(values, weighted, tile_area, halo_rows, coefficient(step_idx))
    sampled = subsample(values)
    weights = subsample(tile_area[:, None])[:, 0].reshape(-1)
    snap_rows = jnp.transpose(sampled, (1, 0, 2)).reshape(snap_count, -1)
    cell_count = tile_ids.shape[0] * sampled.shape[2]
    weighted_rows = snap_rows * weights
    partial_gram = jnp.dot(
        weighted_rows,
        lax.all_gather(snap_rows, "tm", axis=0, tiled=True).T,
        precision=lax.Precision.HIGHEST,
        preferred_element_type=jnp.float32,
    )
    gram_rows = lax.psum(partial_gram, "space")
    return gram_rows / cell_count


def solution(mesh):
    placed = (P("space", "tm", None), P(), P(), P())
    return jax.shard_map(body, mesh=mesh, in_specs=placed, out_specs=P("tm", None), check_vma=False)
```

profile of v0, /device:TPU:0, one launch (start us, length us, event | category | flops | bytes accessed | tf_op | source)
XLA Modules:
  0.0 2812.5 jit_solution(17650007701592591141)
XLA Ops:
  8.2 2.5 gather_fusion
  12.6 38.6 %broadcast_multiply_fusion.3 = f32[12,32,36864]{2,1,0:T(8,128)} fusion(f32[12,32,36864]{2,1,0:T(8,128)} %param.6, f32[12,36864]{1,0:T(8,128)S(1)} %broadcast_select_fusion.1), kind=kLoop, calls=%fused_computation.44 | loop fusion | flops 14155776 | bytes 115015680 | tf_op jit(solution)/shard_map/mul | solution.py:68
  51.2 20.6 slice.196
  71.8 20.7 slice.195
  95.4 74.4 %fusion.46 = (f32[12,32,36672]{2,1,0:T(8,128)}, f32[12,32,36672]{2,1,0:T(8,128)}) fusion(f32[12,32,36864]{2,1,0:T(8,128)} %broadcast_multiply_fusion.3), kind=kLoop, calls=%fused_computation.117 | loop fusion | bytes 225312768 | tf_op jit(solution)/shard_map/slice | solution.py:40
  172.9 73.9 %fusion.48 = (f32[12,32,36863]{2,1,0:T(8,128)}, f32[12,32,36863]{2,1,0:T(8,128)}) fusion(f32[12,32,36864]{2,1,0:T(8,128)} %broadcast_multiply_fusion.3), kind=kLoop, calls=%fused_computation.119 | loop fusion | bytes 226486272 | tf_op jit(solution)/shard_map/slice | solution.py:42
  246.7 27.7 all-gather.6.cloned.1.call-done
  274.4 11.9 copy.15
  286.3 6.4 gather_fusion.1
  294.3 2.2 reverse
  298.6 24.1 broadcast_in_dim.110
  322.7 70.2 %reshape.114 = f32[12,32,36864]{2,1,0:T(8,128)} reshape(f32[12,32,192,192]{3,2,1,0:T(8,128)} %broadcast_in_dim.110) | data formatting | bytes 113246208 | tf_op jit(solution)/shard_map/reshape | solution.py:45
  392.8 24.0 broadcast_in_dim.108
  416.8 70.3 %reshape.113 = f32[12,32,36864]{2,1,0:T(8,128)} reshape(f32[12,32,192,192]{3,2,1,0:T(8,128)} %broadcast_in_dim.108) | data formatting | bytes 113246208 | tf_op jit(solution)/shard_map/reshape | solution.py:44
  487.1 159.0 %broadcast_multiply_fusion.2 = (f32[12,32,36864]{2,1,0:T(8,128)}, f32[12,32,36864]{2,1,0:T(8,128)}) fusion(f32[12,36864]{1,0:T(8,128)S(1)} %copy-done.3, f32[12,32,36864]{2,1,0:T(8,128)} %param.6, f32[12,32,36864]{2,1,0:T(8,128)} %reshape.114, f32[12,32,1]{2,1,0:T(8,128)} %get-tuple-element.41, f32[12,32,36863]{2,1,0:T(8,128)} %get-tuple-element.43, ...), kind=kLoop, calls=%fused_computation.43 | loop fusion | flops 226492416 | bytes 511451136 | tf_op jit(solution)/shard_map/mul | solution.py:68
  646.2 21.0 slice.212
  667.2 20.7 slice.211
  690.6 75.2 %fusion.43 = (f32[12,32,36672]{2,1,0:T(8,128)}, f32[12,32,36672]{2,1,0:T(8,128)}) fusion(f32[12,32,36864]{2,1,0:T(8,128)} %get-tuple-element.10), kind=kLoop, calls=%fused_computation.114 | loop fusion | bytes 225312768 | tf_op jit(solution)/shard_map/slice | solution.py:40
  767.7 73.9 %fusion.45 = (f32[12,32,36863]{2,1,0:T(8,128)}, f32[12,32,36863]{2,1,0:T(8,128)}) fusion(f32[12,32,36864]{2,1,0:T(8,128)} %get-tuple-element.10), kind=kLoop, calls=%fused_computation.116 | loop fusion | bytes 226486272 | tf_op jit(solution)/shard_map/slice | solution.py:42
  841.6 23.7 all-gather.8.cloned.1.call-done
  865.3 11.8 copy.16
  877.1 6.5 gather_fusion.2
  885.2 2.2 reverse.1
  889.5 24.1 broadcast_in_dim.112
  913.6 70.2 %reshape.118 = f32[12,32,36864]{2,1,0:T(8,128)} reshape(f32[12,32,192,192]{3,2,1,0:T(8,128)} %broadcast_in_dim.112) | data formatting | bytes 113246208 | tf_op jit(solution)/shard_map/reshape | solution.py:45
  983.7 24.0 broadcast_in_dim.111
  1007.7 70.3 %reshape.117 = f32[12,32,36864]{2,1,0:T(8,128)} reshape(f32[12,32,192,192]{3,2,1,0:T(8,128)} %broadcast_in_dim.111) | data formatting | bytes 113246208 | tf_op jit(solution)/shard_map/reshape | solution.py:44
  1078.0 159.0 %broadcast_multiply_fusion.1 = (f32[12,32,36864]{2,1,0:T(8,128)}, f32[12,32,36864]{2,1,0:T(8,128)}) fusion(f32[12,36864]{1,0:T(8,128)S(1)} %copy-done.4, f32[12,32,36864]{2,1,0:T(8,128)} %get-tuple-element.11, f32[12,32,36864]{2,1,0:T(8,128)} %reshape.118, f32[12,32,1]{2,1,0:T(8,128)} %get-tuple-element.33, f32[12,32,36863]{2,1,0:T(8,128)} %get-tuple-element.35, ...), kind=kLoop, calls=%fused_computation.42 | loop fusion | flops 226492416 | bytes 511451136 | tf_op jit(solution)/shard_map/mul | solution.py:68
  1237.1 20.8 slice.226
  1257.9 20.7 slice.225
  1281.2 75.2 %fusion.40 = (f32[12,32,36672]{2,1,0:T(8,128)}, f32[12,32,36672]{2,1,0:T(8,128)}) fusion(f32[12,32,36864]{2,1,0:T(8,128)} %get-tuple-element.8), kind=kLoop, calls=%fused_computation.111 | loop fusion | bytes 225312768 | tf_op jit(solution)/shard_map/slice | solution.py:40
  1358.3 73.9 %fusion.42 = (f32[12,32,36863]{2,1,0:T(8,128)}, f32[12,32,36863]{2,1,0:T(8,128)}) fusion(f32[12,32,36864]{2,1,0:T(8,128)} %get-tuple-element.8), kind=kLoop, calls=%fused_computation.113 | loop fusion | bytes 226486272 | tf_op jit(solution)/shard_map/slice | solution.py:42
  1432.3 23.7 all-gather.10.cloned.1.call-done
  1456.0 11.8 copy.17
  1467.8 6.5 gather_fusion.3
  1475.9 2.2 reverse.2
  1480.2 24.1 broadcast_in_dim.114
  1504.3 70.2 %reshape.122 = f32[12,32,36864]{2,1,0:T(8,128)} reshape(f32[12,32,192,192]{3,2,1,0:T(8,128)} %broadcast_in_dim.114) | data formatting | bytes 113246208 | tf_op jit(solution)/shard_map/reshape | solution.py:45
  1574.5 24.0 broadcast_in_dim.113
  1598.5 70.3 %reshape.121 = f32[12,32,36864]{2,1,0:T(8,128)} reshape(f32[12,32,192,192]{3,2,1,0:T(8,128)} %broadcast_in_dim.113) | data formatting | bytes 113246208 | tf_op jit(solution)/shard_map/reshape | solution.py:44
  1668.8 159.1 %broadcast_multiply_fusion = (f32[12,32,36864]{2,1,0:T(8,128)}, f32[12,32,36864]{2,1,0:T(8,128)}) fusion(f32[12,36864]{1,0:T(8,128)S(1)} %copy-done.5, f32[12,32,36864]{2,1,0:T(8,128)} %get-tuple-element.9, f32[12,32,36864]{2,1,0:T(8,128)} %reshape.122, f32[12,32,1]{2,1,0:T(8,128)} %get-tuple-element.25, f32[12,32,36863]{2,1,0:T(8,128)} %get-tuple-element.27, ...), kind=kLoop, calls=%fused_computation.41 | loop fusion | flops 226492416 | bytes 511451136 | tf_op jit(solution)/shard_map/mul | solution.py:68
  1827.9 21.0 slice.240
  1848.9 20.7 slice.239
  1872.4 75.3 %fusion.39 = (f32[12,32,36672]{2,1,0:T(8,128)}, f32[12,32,36672]{2,1,0:T(8,128)}) fusion(f32[12,32,36864]{2,1,0:T(8,128)} %get-tuple-element.6), kind=kLoop, calls=%fused_computation.110 | loop fusion | bytes 225312768 | tf_op jit(solution)/shard_map/slice | solution.py:41
  1949.5 73.8 %fusion.37 = (f32[12,32,36863]{2,1,0:T(8,128)}, f32[12,32,36863]{2,1,0:T(8,128)}) fusion(f32[12,32,36864]{2,1,0:T(8,128)} %get-tuple-element.6), kind=kLoop, calls=%fused_computation.108 | loop fusion | bytes 226486272 | tf_op jit(solution)/shard_map/slice | solution.py:43
  2023.3 23.8 all-gather.12.cloned.1.call-done
  2047.1 11.8 copy.18
  2058.9 6.5 gather_fusion.4
  2066.9 2.2 reverse.3
  2071.2 24.1 broadcast_in_dim.116
  2095.3 70.2 %reshape.126 = f32[12,32,36864]{2,1,0:T(8,128)} reshape(f32[12,32,192,192]{3,2,1,0:T(8,128)} %broadcast_in_dim.116) | data formatting | bytes 113246208 | tf_op jit(solution)/shard_map/reshape | solution.py:45
  2165.5 24.0 broadcast_in_dim.115
  2189.5 70.3 %reshape.125 = f32[12,32,36864]{2,1,0:T(8,128)} reshape(f32[12,32,192,192]{3,2,1,0:T(8,128)} %broadcast_in_dim.115) | data formatting | bytes 113246208 | tf_op jit(solution)/shard_map/reshape | solution.py:44
  2259.8 138.6 %fusion.23 = f32[12,32,36864]{2,1,0:T(8,128)} fusion(f32[12,32,36864]{2,1,0:T(8,128)} %get-tuple-element.7, f32[12,32,36672]{2,1,0:T(8,128)} %get-tuple-element.19, f32[12,32,192]{2,1,0:T(8,128)S(1)} %get-tuple-element.49, f32[12,32,192]{2,1,0:T(8,128)S(1)} %get-tuple-element.48, f32[12,32,36672]{2,1,0:T(8,128)} %get-tuple-element.18, ...), kind=kLoop, calls=%fused_computation.38 | loop fusion | flops 212336640 | bytes 454828032 | tf_op jit(solution)/shard_map/add | solution.py:47
  2398.3 69.5 %reshape.127 = f32[12,32,192,192]{3,2,1,0:T(8,128)} reshape(f32[12,32,36864]{2,1,0:T(8,128)} %fusion.23) | data formatting | bytes 113246208 | tf_op jit(solution)/shard_map/reshape | solution.py:53
  2467.9 181.5 %slice.251 = f32[12,32,48,48]{3,2,1,0:T(8,128)} slice(f32[12,32,192,192]{3,2,1,0:T(8,128)} %reshape.127), slice={[0:12:1], [0:32:1], [1:192:4], [1:192:4]} | slice | bytes 7077888 | tf_op jit(solution)/shard_map/slice | solution.py:53
  2649.4 8.4 reshape.128
  2657.9 4.1 copy.20
  2661.9 3.4 gather.10
  2665.3 3.7 broadcast_select_fusion
  2669.1 7.9 slice.252
  2677.1 74.2 %all-gather.14.cloned.1.call-done = f32[128,27648]{1,0:T(8,128)} async-done(((f32[32,27648]{1,0:T(8,128)}), f32[128,27648]{1,0:T(8,128)}) %all-gather.14.cloned.1.call-update) | async-done | bytes 14155792 | tf_op jit(solution)/shard_map/all_gather | solution.py:79
  2751.3 16.7 fusion.24
  2768.1 37.1 %psum.7 = f32[32,128]{1,0:T(8,128)S(1)} all-reduce(f32[32,128]{1,0:T(8,128)S(1)} %fusion.24), channel_id=1, replica_groups=mesh['space'=8,'tm'=4] {'space'}, use_global_device_ids=true, to_apply=%region_0.2 | all-reduce | flops 4096 | bytes 32768 | tf_op jit(solution)/shard_map/psum | solution.py:83
  (110 shorter events, 38.7 us)
Async XLA Ops:
  6.5 1.7 copy-start
  6.5 267.9 %all-gather.6.cloned.1.call-start = ((), (), s32[]{:S(2)}) async-start(), calls=%async_computation | async-start | bytes 14155776 | tf_op jit(solution)/shard_map/all_gather | solution.py:69
  7.4 5.1 copy-start.29
  12.6 38.6 %copy-start.2 = (f32[12,36864]{1,0:T(8,128)}, f32[12,36864]{1,0:T(8,128)S(1)}, u32[]{:S(2)}) copy-start(f32[12,36864]{1,0:T(8,128)S(1)} %broadcast_select_fusion.1) | copy-start | bytes 5308420
  95.1 74.6 %copy-start.28 = (s32[3,96,4]{1,2,0:T(4,128)S(1)}, s32[3,96,4]{1,2,0:T(4,128)}, u32[]{:S(2)}) copy-start(s32[3,96,4]{1,2,0:T(4,128)} %param.9) | copy-start | bytes 13828
  95.1 770.2 %all-gather.8.cloned.1.call-start = ((), (), s32[]{:S(2)}) async-start(), calls=%async_computation.1 | async-start | bytes 14155776 | tf_op jit(solution)/shard_map/all_gather | solution.py:69
  169.9 126.6 %copy-start.19 = (pred[12,4]{1,0:T(8,128)(4,1)}, pred[12,4]{1,0:T(8,128)(4,1)S(1)}, u32[]{:S(2)}) copy-start(pred[12,4]{1,0:T(8,128)(4,1)S(1)} %copy.13) | copy-start | bytes 148
  170.2 116.1 %copy-start.23 = (s32[1024]{0:T(1024)}, s32[1024]{0:T(1024)S(1)}, u32[]{:S(2)}) copy-start(s32[1024]{0:T(1024)S(1)} %pad_clamp_fusion) | copy-start | bytes 12292
  170.2 122.5 %copy-start.24 = (pred[48]{0:T(512)(128)(4,1)}, pred[48]{0:T(512)(128)(4,1)S(1)}, u32[]{:S(2)}) copy-start(pred[48]{0:T(512)(128)(4,1)S(1)} %compare_and_fusion) | copy-start | bytes 148
  416.8 70.3 %copy-start.3 = (f32[12,36864]{1,0:T(8,128)S(1)}, f32[12,36864]{1,0:T(8,128)}, u32[]{:S(2)}) copy-start(f32[12,36864]{1,0:T(8,128)} %copy-done.2) | copy-start | bytes 5308420
  416.8 70.3 %copy-start.7 = (pred[36864]{0:T(1024)(128)(4,1)S(1)}, pred[36864]{0:T(1024)(128)(4,1)}, u32[]{:S(2)}) copy-start(pred[36864]{0:T(1024)(128)(4,1)} %get-tuple-element.62) | copy-start | bytes 110596
  416.8 70.3 %copy-start.11 = (pred[36864]{0:T(1024)(128)(4,1)S(1)}, pred[36864]{0:T(1024)(128)(4,1)}, u32[]{:S(2)}) copy-start(pred[36864]{0:T(1024)(128)(4,1)} %get-tuple-element.63) | copy-start | bytes 110596
  416.8 70.3 %copy-start.15 = (f32[12,32,1]{2,1,0:T(8,128)S(1)}, f32[12,32,1]{2,1,0:T(8,128)}, u32[]{:S(2)}) copy-start(f32[12,32,1]{2,1,0:T(8,128)} %get-tuple-element.40) | copy-start | bytes 4612
  690.5 765.4 %all-gather.10.cloned.1.call-start = ((), (), s32[]{:S(2)}) async-start(), calls=%async_computation.2 | async-start | bytes 14155776 | tf_op jit(solution)/shard_map/all_gather | solution.py:69
  767.6 116.0 %copy-start.25 = (pred[48]{0:T(512)(128)(4,1)S(1)}, pred[48]{0:T(512)(128)(4,1)}, u32[]{:S(2)}) copy-start(pred[48]{0:T(512)(128)(4,1)} %copy-done.24) | copy-start | bytes 148
  767.6 119.7 %copy-start.20 = (pred[12,4]{1,0:T(8,128)(4,1)S(1)}, pred[12,4]{1,0:T(8,128)(4,1)}, u32[]{:S(2)}) copy-start(pred[12,4]{1,0:T(8,128)(4,1)} %copy-done.19) | copy-start | bytes 148
  1007.7 70.3 %copy-start.4 = (f32[12,36864]{1,0:T(8,128)S(1)}, f32[12,36864]{1,0:T(8,128)}, u32[]{:S(2)}) copy-start(f32[12,36864]{1,0:T(8,128)} %copy-done.2) | copy-start | bytes 5308420
  1007.7 70.3 %copy-start.8 = (pred[36864]{0:T(1024)(128)(4,1)S(1)}, pred[36864]{0:T(1024)(128)(4,1)}, u32[]{:S(2)}) copy-start(pred[36864]{0:T(1024)(128)(4,1)} %get-tuple-element.62) | copy-start | bytes 110596
  1007.7 70.3 %copy-start.12 = (pred[36864]{0:T(1024)(128)(4,1)S(1)}, pred[36864]{0:T(1024)(128)(4,1)}, u32[]{:S(2)}) copy-start(pred[36864]{0:T(1024)(128)(4,1)} %get-tuple-element.63) | copy-start | bytes 110596
  1007.7 70.3 %copy-start.16 = (f32[12,32,1]{2,1,0:T(8,128)S(1)}, f32[12,32,1]{2,1,0:T(8,128)}, u32[]{:S(2)}) copy-start(f32[12,32,1]{2,1,0:T(8,128)} %get-tuple-element.32) | copy-start | bytes 4612
  1281.2 765.9 %all-gather.12.cloned.1.call-start = ((), (), s32[]{:S(2)}) async-start(), calls=%async_computation.3 | async-start | bytes 14155776 | tf_op jit(solution)/shard_map/all_gather | solution.py:69
  1358.3 116.0 %copy-start.26 = (pred[48]{0:T(512)(128)(4,1)S(1)}, pred[48]{0:T(512)(128)(4,1)}, u32[]{:S(2)}) copy-start(pred[48]{0:T(512)(128)(4,1)} %copy-done.24) | copy-start | bytes 148
  1358.3 119.8 %copy-start.21 = (pred[12,4]{1,0:T(8,128)(4,1)S(1)}, pred[12,4]{1,0:T(8,128)(4,1)}, u32[]{:S(2)}) copy-start(pred[12,4]{1,0:T(8,128)(4,1)} %copy-done.19) | copy-start | bytes 148
  1598.4 70.4 %copy-start.5 = (f32[12,36864]{1,0:T(8,128)S(1)}, f32[12,36864]{1,0:T(8,128)}, u32[]{:S(2)}) copy-start(f32[12,36864]{1,0:T(8,128)} %copy-done.2) | copy-start | bytes 5308420
  1598.4 70.4 %copy-start.9 = (pred[36864]{0:T(1024)(128)(4,1)S(1)}, pred[36864]{0:T(1024)(128)(4,1)}, u32[]{:S(2)}) copy-start(pred[36864]{0:T(1024)(128)(4,1)} %get-tuple-element.62) | copy-start | bytes 110596
  1598.4 70.4 %copy-start.13 = (pred[36864]{0:T(1024)(128)(4,1)S(1)}, pred[36864]{0:T(1024)(128)(4,1)}, u32[]{:S(2)}) copy-start(pred[36864]{0:T(1024)(128)(4,1)} %get-tuple-element.63) | copy-start | bytes 110596
  1598.4 70.4 %copy-start.17 = (f32[12,32,1]{2,1,0:T(8,128)S(1)}, f32[12,32,1]{2,1,0:T(8,128)}, u32[]{:S(2)}) copy-start(f32[12,32,1]{2,1,0:T(8,128)} %get-tuple-element.24) | copy-start | bytes 4612
  1872.3 879.0 %all-gather.14.cloned.1.call-start = ((), (), s32[]{:S(2)}) async-start(), calls=%async_computation.4 | async-start | bytes 17694720 | tf_op jit(solution)/shard_map/all_gather | solution.py:79
  1949.5 115.9 %copy-start.27 = (pred[48]{0:T(512)(128)(4,1)S(1)}, pred[48]{0:T(512)(128)(4,1)}, u32[]{:S(2)}) copy-start(pred[48]{0:T(512)(128)(4,1)} %copy-done.24) | copy-start | bytes 148
  1949.5 119.6 %copy-start.22 = (pred[12,4]{1,0:T(8,128)(4,1)S(1)}, pred[12,4]{1,0:T(8,128)(4,1)}, u32[]{:S(2)}) copy-start(pred[12,4]{1,0:T(8,128)(4,1)} %copy-done.19) | copy-start | bytes 148
  2189.4 70.3 %copy-start.6 = (f32[12,36864]{1,0:T(8,128)S(1)}, f32[12,36864]{1,0:T(8,128)}, u32[]{:S(2)}) copy-start(f32[12,36864]{1,0:T(8,128)} %copy-done.2) | copy-start | bytes 5308420
  2189.4 70.3 %copy-start.10 = (pred[36864]{0:T(1024)(128)(4,1)S(1)}, pred[36864]{0:T(1024)(128)(4,1)}, u32[]{:S(2)}) copy-start(pred[36864]{0:T(1024)(128)(4,1)} %get-tuple-element.62) | copy-start | bytes 110596
  2189.4 70.3 %copy-start.14 = (pred[36864]{0:T(1024)(128)(4,1)S(1)}, pred[36864]{0:T(1024)(128)(4,1)}, u32[]{:S(2)}) copy-start(pred[36864]{0:T(1024)(128)(4,1)} %get-tuple-element.63) | copy-start | bytes 110596
  2189.4 70.3 %copy-start.18 = (f32[12,32,1]{2,1,0:T(8,128)S(1)}, f32[12,32,1]{2,1,0:T(8,128)}, u32[]{:S(2)}) copy-start(f32[12,32,1]{2,1,0:T(8,128)} %get-tuple-element.16) | copy-start | bytes 4612
  2398.3 267.0 %copy-start.30 = (pred[12]{0:T(512)(128)(4,1)S(1)}, pred[12]{0:T(512)(128)(4,1)}, u32[]{:S(2)}) copy-start(pred[12]{0:T(512)(128)(4,1)} %copy-done.29) | copy-start | bytes 40
  2398.3 407.4 %copy-start.1 = (f32[16,36864]{1,0:T(8,128)S(1)}, f32[16,36864]{1,0:T(8,128)}, u32[]{:S(2)}) copy-start(f32[16,36864]{1,0:T(8,128)} %param.7) | copy-start | bytes 7077892
Sparse Core Ops, SparseCore 0:
  95.2 179.1 all-gather.5
  690.7 174.6 all-gather.7
  1281.3 174.6 all-gather.9
  1872.4 174.6 all-gather.11
  2662.1 89.2 all-gather.13
where the time goes:
time: 2830 us; the launch traced here: 2810 us
  local copies, waits for them, and re-layouts  1890 us (67%)
  other arithmetic  682 us (24%)
  waiting for transfers between devices  173 us (6%)
  blocking collectives  37.1 us (1%)
    mul x4, other arithmetic, body(): weighted = tile_area[:, None] * values  516 us
    reshape x4, local copies, waits for them, and re-layouts, smooth_step(): jnp.repeat(halo_rows[:, 2], TILE, axis=2)  281 us
    reshape x4, local copies, waits for them, and re-layouts, smooth_step(): jnp.repeat(halo_rows[:, 3], TILE, axis=2)  281 us
    slice x3, local copies, waits for them, and re-layouts, smooth_step(): weighted[:, :, :-TILE]  225 us
    slice x3, local copies, waits for them, and re-layouts, smooth_step(): weighted[:, :, :-1]  222 us
    slice x2, local copies, waits for them, and re-layouts, subsample(): values.reshape(values.shape[0], values.shape[1], TILE, TILE)  189 us
    add x1, other arithmetic, smooth_step(): values + factor * (upper_nb + lower_nb + left_nb + right_nb - 4.0 * weigh...  139 us
    all_gather x4, waiting for transfers between devices, body(): lax.all_gather(edge_strips(weighted), 'space', axis=0, tiled=True)  98.9 us
  transfers between devices with their start and end apart: 5, of which 5 were waited for; matrix products, arithmetic and copies ran while one was open for 22% of the time, Pallas kernels for 0%

commit v1 on v0

v1 whole, which is shorter than its diff:
```python
import functools
import jax
import jax.numpy as jnp
import ml_dtypes
import numpy as np
from jax import lax
from jax.experimental import pallas as pl
from jax.experimental.pallas import tpu as pltpu
from jax.sharding import PartitionSpec as P

STRIDE = 4
STEPS = 4
TILE = 192
SIDE = TILE // STRIDE
ROWS = 2 * STRIDE
CHUNKS = TILE // ROWS
DEPTH = ROWS * TILE
RIM = 4 * TILE
LANES = 128
HALF = 64
F32, BF16 = jnp.float32, jnp.bfloat16
VMEM_LIMIT = 56 * 1024 * 1024


def coefficient(step_idx):
    return 0.12 + 0.1 * step_idx / max(STEPS - 1, 1)


def stencil_taps():
    taps = np.zeros((2 * STEPS + 1, 2 * STEPS + 1))
    taps[STEPS, STEPS] = 1.0
    for step_idx in range(STEPS):
        padded = np.pad(taps, 1)
        lap = (
            padded[:-2, 1:-1] + padded[2:, 1:-1] + padded[1:-1, :-2] + padded[1:-1, 2:] - 4 * taps
        )
        taps = taps + coefficient(step_idx) * lap
    return taps


TAPS = stencil_taps()
CORNER = 3.0 * float(np.prod([coefficient(k) for k in range(STEPS)]))


def response(row, col, first_row, row_count):
    plane = np.zeros((row_count, TILE))
    for d_row in range(-STEPS, STEPS + 1):
        for d_col in range(-STEPS, STEPS + 1):
            at_row, at_col = row + d_row - first_row, col + d_col
            if 0 <= at_row < row_count and 0 <= at_col < TILE:
                plane[at_row, at_col] = TAPS[d_row + STEPS, d_col + STEPS]
    return plane.reshape(-1)


def split_const(matrix):
    high = matrix.astype(ml_dtypes.bfloat16)
    low = (matrix - high.astype(np.float64)).astype(ml_dtypes.bfloat16)
    return high, low


def along(variant, index):
    return TILE - 2 - STRIDE * index if variant % 2 else 1 + STRIDE * index


def beyond(variant):
    return 3 if variant // 2 else 2


def chunk_matrix():
    matrix = np.zeros((DEPTH, 2 * LANES))

    def put(lane, slot, row, col):
        matrix[:, lane] = response(row, col, 0, ROWS)
        other = row + ROWS if slot == 0 else row - ROWS
        matrix[:, LANES + lane] = response(other, col, 0, ROWS)

    for slot in range(2):
        for index in range(SIDE):
            put(slot * SIDE + index, slot, 1 + STRIDE * slot, 1 + STRIDE * index)
        for side in range(2):
            for variant in range(4):
                col = TILE - 1 + beyond(variant) if side else -beyond(variant)
                row = (2 if variant % 2 else 1) + STRIDE * slot
                put(2 * SIDE + side * 8 + variant * 2 + slot, slot, row, col)
    return matrix


def rim_matrices():
    upper = np.zeros((RIM, 4 * LANES))
    lower = np.zeros((RIM, 4 * LANES))
    for variant in range(4):
        base = variant * LANES
        for index in range(SIDE):
            col = along(variant, index)
            upper[:, base + index] = response(-beyond(variant), col, 0, 4)
            lower[:, base + HALF + index] = response(
                TILE - 1 + beyond(variant), col, TILE - 4, 4
            )
        upper[0, base + SIDE] = 1.0
        upper[TILE - 1, base + SIDE + 1] = 1.0
        lower[3 * TILE, base + HALF + SIDE] = 1.0
        lower[4 * TILE - 1, base + HALF + SIDE + 1] = 1.0
    return upper, lower


def order_matrix():
    matrix = np.zeros((CHUNKS * 16, 4 * LANES))
    for chunk in range(CHUNKS):
        for side in range(2):
            for variant in range(4):
                for slot in range(2):
                    index = 2 * chunk + slot
                    place = SIDE - 1 - index if variant % 2 else index
                    source = chunk * 16 + side * 8 + variant * 2 + slot
                    matrix[source, variant * LANES + side * HALF + place] = 1.0
    return matrix.astype(ml_dtypes.bfloat16)


def place_matrix():
    matrix = np.zeros((CHUNKS, 2 * LANES, LANES))
    for index in range(SIDE):
        chunk, slot = index // 2, index % 2
        matrix[0, index, index] = 1.0
        matrix[CHUNKS - 1, HALF + index, SIDE + index] = 1.0
        matrix[chunk, LANES + index, slot * SIDE] = 1.0
        matrix[chunk, LANES + HALF + index, slot * SIDE + SIDE - 1] = 1.0
    for lane in (SIDE, SIDE + 1, HALF + SIDE, HALF + SIDE + 1):
        matrix[0, lane, 0] = 1.0
    return matrix.astype(ml_dtypes.bfloat16)


def split(x):
    high = x.astype(BF16)
    return high, (x - high.astype(F32)).astype(BF16)


def dot(a, b):
    return jnp.dot(a, b, preferred_element_type=F32)


def dot3(a_high, a_low, b_high, b_low):
    return dot(a_high, b_high) + dot(a_low, b_high) + dot(a_high, b_low)


def stencil_kernel(
    tiles, snaps, slots, faces,
    first_ref, ids_ref, table_ref,
    x_ref, area_ref, main_h, main_l, up_h, up_l, down_h, down_l, order_ref,
    out_ref, send_ref,
    high, low, carry, edges, rims,
):
    step = pl.program_id(0)
    first = first_ref[0]
    rows = tiles * snaps
    for t in range(tiles):
        face = lax.rem(ids_ref[first + t], faces)
        part = pl.ds(t * snaps, snaps)
        h, l = split(x_ref[t] * area_ref[pl.ds(face, 1), :])
        high[part, :] = h
        low[part, :] = l
    lane = lax.broadcasted_iota(jnp.int32, (rows, LANES), 1)
    from_before = (lane < SIDE) | ((lane >= 2 * SIDE) & (lane % 2 == 0))
    is_edge = (lane >= 2 * SIDE) & (lane < 2 * SIDE + 16)

    def collect(chunk, value):
        shift = lax.rem(16 * lax.rem(chunk, 8) + LANES - 2 * SIDE, LANES)
        block = lax.div(chunk, 8)
        edges[block] = edges[block] + pltpu.roll(jnp.where(is_edge, value, 0.0), shift, 1)

    @pl.when(step == 0)
    def _():
        carry[...] = jnp.zeros_like(carry)
        edges[...] = jnp.zeros_like(edges)
        rims[...] = dot3(high[:, :RIM], low[:, :RIM], up_h[...], up_l[...])

    result = dot3(high[...], low[...], main_h[...], main_l[...])
    own, other = result[:, :LANES], result[:, LANES:]

    @pl.when(step > 0)
    def _():
        done = out_ref[step - 1] + jnp.where(from_before, 0.0, other)
        out_ref[step - 1] = done
        collect(step - 1, done)

    own = own + jnp.where(from_before, carry[...], 0.0)
    out_ref[step] = own
    carry[...] = other

    @pl.when(step == CHUNKS - 1)
    def _():
        collect(step, own)
        rims[...] = rims[...] + dot3(
            high[:, DEPTH - RIM :], low[:, DEPTH - RIM :], down_h[...], down_l[...]
        )
        sides = jnp.zeros((rows, 4 * LANES), F32)
        for block in range(CHUNKS * 16 // LANES):
            h, l = split(edges[block])
            matrix = order_ref[block * LANES : (block + 1) * LANES, :]
            sides = sides + dot(h, matrix) + dot(l, matrix)
        low_half = lane[:snaps] < HALF
        for t in range(tiles):
            part = slice(t * snaps, (t + 1) * snaps)
            for pair, source in ((0, rims[part, :]), (1, sides[part, :])):
                chosen = jnp.zeros((snaps, LANES), F32)
                at = (first + t) * 4 + 2 * pair
                kind = [
                    2 * lax.rem(table_ref[slots * 4 + at + k], 2) + table_ref[slots * 8 + at + k]
                    for k in range(2)
                ]
                for variant in range(4):
                    block = source[:, variant * LANES : (variant + 1) * LANES]
                    wanted = jnp.where(
                        low_half,
                        (kind[0] == variant).astype(jnp.int32),
                        (kind[1] == variant).astype(jnp.int32),
                    )
                    chosen = jnp.where(wanted == 1, block, chosen)
                send_ref[t, pair] = chosen


def halo_kernel(
    tiles, snaps, slots, faces, per_step,
    first_ref, ids_ref, table_ref,
    strips_ref, sums_ref, root_ref, place_ref,
    out_ref,
    high, low,
):
    step = pl.program_id(0)
    first = first_ref[0]
    lane = lax.broadcasted_iota(jnp.int32, (snaps, LANES), 1)

    def near(slot, edge):
        at = slot * 4 + edge
        return table_ref[at], table_ref[slots * 4 + at], table_ref[slots * 8 + at]

    def corner(slot, edge):
        mid, mid_edge, mid_flip = near(slot, edge)
        other_edge = jnp.where(mid_edge < 2, 2, 0) + mid_flip
        end = lax.rem(mid_edge, 2)
        far, far_edge, far_flip = near(mid, other_edge)
        far_end = jnp.where(far_flip == 1, 1 - end, end)
        side = lax.rem(far_edge, 2)
        row_end = jnp.where(far_edge < 2, side, far_end)
        col_end = jnp.where(far_edge < 2, far_end, side)
        value = strips_ref[far, 0]
        return jnp.where(lane == SIDE + col_end + HALF * row_end, value, 0.0)

    @pl.when(step == 0)
    def _():
        for t in range(tiles):
            slot = first + t
            part = pl.ds(t * snaps, snaps)
            for pair in range(2):
                strips = []
                for k in range(2):
                    far, far_edge, _ = near(slot, 2 * pair + k)
                    value = strips_ref[far, lax.div(far_edge, 2)]
                    rolled = pltpu.roll(value, HALF, 1)
                    same = (jnp.zeros((snaps, LANES), jnp.int32) + lax.rem(far_edge, 2)) == k
                    strips.append(jnp.where(same, value, rolled))
                both = jnp.where(lane < HALF, strips[0], strips[1])
                both = jnp.where(lane % HALF < SIDE, both, 0.0)
                if pair == 0:
                    both = both + CORNER * (corner(slot, 0) + corner(slot, 2))
                h, l = split(both)
                high[part, pair * LANES : (pair + 1) * LANES] = h
                low[part, pair * LANES : (pair + 1) * LANES] = l

    for chunk in range(per_step):
        added = dot(high[...], place_ref[chunk]) + dot(low[...], place_ref[chunk])
        for t in range(tiles):
            part = slice(t * snaps, (t + 1) * snaps)
            face = lax.rem(ids_ref[first + t], faces)
            out_ref[chunk, part, :] = (sums_ref[chunk, part, :] + added[part, :]) * root_ref[
                chunk, pl.ds(face, 1), :
            ]


def gram_kernel(tiles, snaps, groups, scale, x_ref, out_ref, main, cross):
    step = pl.program_id(0)

    @pl.when(step == 0)
    def _():
        main[...] = jnp.zeros_like(main)
        cross[...] = jnp.zeros_like(cross)

    dims = (((1,), (1,)), ((), ()))
    count = groups * snaps
    highs, lows = [], []
    for t in range(tiles):
        x = x_ref[:, 0, t * snaps : (t + 1) * snaps, :].reshape(count, LANES)
        h, l = split(x)
        highs.append(h)
        lows.append(l)
    h = jnp.concatenate(highs, axis=1)
    l = jnp.concatenate(lows, axis=1)
    main[...] += lax.dot_general(h, h, dims, preferred_element_type=F32)
    cross[...] += lax.dot_general(h, l, dims, preferred_element_type=F32)

    @pl.when(step == pl.num_programs(0) - 1)
    def _():
        out_ref[...] = (main[...] + cross[...] + cross[...].T) * scale


def full(shape):
    return pl.BlockSpec(shape, lambda c, *_: (0,) * len(shape))


def body(groups, pw_field, cell_area, tile_ids, edge_table):
    tiles, snaps, cells = pw_field.shape
    slots, faces = tile_ids.shape[0], cell_area.shape[0]
    rows = tiles * snaps
    first = (lax.axis_index("space") * tiles).astype(jnp.int32).reshape(1)
    table = edge_table.reshape(-1)
    main_h, main_l = split_const(chunk_matrix())
    upper, lower = rim_matrices()
    up_h, up_l = split_const(upper)
    down_h, down_l = split_const(lower)

    sums, send = pl.pallas_call(
        functools.partial(stencil_kernel, tiles, snaps, slots, faces),
        grid_spec=pltpu.PrefetchScalarGridSpec(
            num_scalar_prefetch=3,
            grid=(CHUNKS,),
            in_specs=[
                pl.BlockSpec((tiles, snaps, DEPTH), lambda c, *_: (0, 0, c)),
                pl.BlockSpec((faces, DEPTH), lambda c, *_: (0, c)),
                full((DEPTH, 2 * LANES)),
                full((DEPTH, 2 * LANES)),
                full((RIM, 4 * LANES)),
                full((RIM, 4 * LANES)),
                full((RIM, 4 * LANES)),
                full((RIM, 4 * LANES)),
                full((CHUNKS * 16, 4 * LANES)),
            ],
            out_specs=[full((CHUNKS, rows, LANES)), full((tiles, 2, snaps, LANES))],
            scratch_shapes=[
                pltpu.VMEM((rows, DEPTH), BF16),
                pltpu.VMEM((rows, DEPTH), BF16),
                pltpu.VMEM((rows, LANES), F32),
                pltpu.VMEM((CHUNKS * 16 // LANES, rows, LANES), F32),
                pltpu.VMEM((rows, 4 * LANES), F32),
            ],
        ),
        out_shape=[
            jax.ShapeDtypeStruct((CHUNKS, rows, LANES), F32),
            jax.ShapeDtypeStruct((tiles, 2, snaps, LANES), F32),
        ],
        compiler_params=pltpu.CompilerParams(vmem_limit_bytes=VMEM_LIMIT),
        name="stencil",
    )(
        first, tile_ids, table, pw_field, cell_area,
        main_h, main_l, up_h, up_l, down_h, down_l, order_matrix(),
    )

    strips = lax.all_gather(send, "space", axis=0, tiled=True)

    sampled = cell_area.reshape(faces, TILE, TILE)[:, 1::STRIDE, 1::STRIDE]
    root = jnp.sqrt(1.0 / sampled).reshape(faces, CHUNKS, 2 * SIDE)
    root = jnp.pad(root, ((0, 0), (0, 0), (0, LANES - 2 * SIDE)))
    root = jnp.transpose(root, (1, 0, 2))

    per_step = CHUNKS // groups
    scaled = pl.pallas_call(
        functools.partial(halo_kernel, tiles, snaps, slots, faces, per_step),
        grid_spec=pltpu.PrefetchScalarGridSpec(
            num_scalar_prefetch=3,
            grid=(groups,),
            in_specs=[
                full((slots, 2, snaps, LANES)),
                pl.BlockSpec((per_step, rows, LANES), lambda c, *_: (c, 0, 0)),
                pl.BlockSpec((per_step, faces, LANES), lambda c, *_: (c, 0, 0)),
                pl.BlockSpec((per_step, 2 * LANES, LANES), lambda c, *_: (c, 0, 0)),
            ],
            out_specs=pl.BlockSpec((per_step, rows, LANES), lambda c, *_: (c, 0, 0)),
            scratch_shapes=[
                pltpu.VMEM((rows, 2 * LANES), BF16),
                pltpu.VMEM((rows, 2 * LANES), BF16),
            ],
        ),
        out_shape=jax.ShapeDtypeStruct((CHUNKS, rows, LANES), F32),
        compiler_params=pltpu.CompilerParams(vmem_limit_bytes=VMEM_LIMIT),
        name="halo",
    )(first, tile_ids, table, strips, sums, root, place_matrix())

    shared = lax.all_to_all(
        scaled.reshape(groups, per_step, rows, LANES), "tm", split_axis=0, concat_axis=0
    )
    count = groups * snaps
    partial_gram = pl.pallas_call(
        functools.partial(gram_kernel, tiles, snaps, groups, 1.0 / (slots * SIDE * SIDE)),
        grid=(per_step,),
        in_specs=[pl.BlockSpec((groups, 1, rows, LANES), lambda c: (0, c, 0, 0))],
        out_specs=pl.BlockSpec((count, count), lambda c: (0, 0)),
        scratch_shapes=[pltpu.VMEM((count, count), F32), pltpu.VMEM((count, count), F32)],
        out_shape=jax.ShapeDtypeStruct((count, count), F32),
        compiler_params=pltpu.CompilerParams(vmem_limit_bytes=VMEM_LIMIT),
        name="gram",
    )(shared)
    total = lax.psum(partial_gram, ("space", "tm"))
    return lax.dynamic_slice_in_dim(total, lax.axis_index("tm") * snaps, snaps, 0)


def solution(mesh):
    placed = (P("space", "tm", None), P(), P(), P())
    return jax.shard_map(
        functools.partial(body, mesh.shape["tm"]),
        mesh=mesh, in_specs=placed, out_specs=P("tm", None), check_vma=False,
    )
```

time: 2830 us -> 321 us (0.11)
  local copies, waits for them, and re-layouts: 1890 us -> 16.1 us
  other arithmetic: 682 us -> 0.12 us
  Pallas kernels: 0 us -> 64.3 us
    slice x22 -> x1, local copies, waits for them, and re-layouts: 959 us -> 9.82 us  [body(): sampled = cell_area.reshape(faces, TILE, TILE)[:, 1::STRIDE, 1::STRIDE]]
    reshape x11 -> x4, local copies, waits for them, and re-layouts: 644 us -> 3.5 us  [the longest x1 2.61 us: body(): sampled = cell_area.reshape(faces, TILE, TILE)[:, 1::STRIDE, 1::STRIDE]]
    mul x4 -> x0, other arithmetic: 516 us -> none  [body(): weighted = tile_area[:, None] * values]
    broadcast_in_dim x8 -> x0, local copies, waits for them, and re-layouts: 192 us -> none  [the longest x4 96.4 us: smooth_step(): jnp.repeat(halo_rows[:, 3], TILE, axis=2)]
    add x2 -> x0, other arithmetic: 139 us -> none  [the longest x1 139 us: smooth_step(): values + factor * (upper_nb + lower_nb + left_nb + right_nb - 4.0 * weigh...]
    all_gather x5 -> x1, waiting for transfers between devices: 173 us -> 49.8 us  [body(): strips = lax.all_gather(send, 'space', axis=0, tiled=True)]
    psum x0 -> x1, waiting for transfers between devices: none -> 115 us  [body(): total = lax.psum(partial_gram, ('space', 'tm'))]
    pallas_call x0 -> x3, Pallas kernels: none -> 64.3 us  [the longest x1 48.9 us: body(): pl.pallas_call(functools.partial(stencil_kernel, tiles, snaps, slots, fac...]
  transfers between devices with their start and end apart: 5 -> 2, of which waited for: 5 -> 2; matrix products, arithmetic and copies ran while one was open for 22% -> 4% of each run, Pallas kernels for 0% -> 0%
where the time goes in v1:
time: 321 us; the launch traced here: 319 us
  waiting for transfers between devices  165 us (51%)
  Pallas kernels  64.3 us (20%)
  blocking collectives  59.8 us (19%)
  local copies, waits for them, and re-layouts  16.1 us (5%)
  between operations  13.5 us (4%)
    psum x1, waiting for transfers between devices, body(): total = lax.psum(partial_gram, ('space', 'tm'))  115 us
    all_to_all x1, blocking collectives, body(): lax.all_to_all(scaled.reshape(groups, per_step, rows, LANES), 'tm', split...  59.8 us
    all_gather x1, waiting for transfers between devices, body(): strips = lax.all_gather(send, 'space', axis=0, tiled=True)  49.8 us
    pallas_call x1, Pallas kernels, body(): pl.pallas_call(functools.partial(stencil_kernel, tiles, snaps, slots, fac...  48.9 us
    slice x1, local copies, waits for them, and re-layouts, body(): sampled = cell_area.reshape(faces, TILE, TILE)[:, 1::STRIDE, 1::STRIDE]  9.82 us
    pallas_call x1, Pallas kernels, body(): pl.pallas_call(functools.partial(halo_kernel, tiles, snaps, slots, faces,...  9.63 us
  transfers between devices with their start and end apart: 2, of which 2 were waited for; matrix products, arithmetic and copies ran while one was open for 4% of the time, Pallas kernels for 0%

profile of v1, /device:TPU:0, one launch (start us, length us, event | category | flops | bytes accessed | tf_op | source)
XLA Modules:
  0.0 319.1 jit_solution(4885478031001110643)
XLA Ops:
  6.5 0.0 all-gather.2.cloned.1.call-start
  6.5 0.8 copy.15
  7.3 0.7 reshape.16.table_ref
  8.1 0.0 copy-start
  8.1 48.9 %stencil.1 = (f32[24,384,128]{2,1,0:T(8,128)}, f32[12,2,32,128]{3,2,1,0:T(8,128)}) custom-call(s32[1]{0:T(128)} %bitcast.first_ref, s32[96]{0:T(128)} %ids_ref.3, s32[1152]{0:T(1024)} %reshape.16.table_ref, f32[12,32,36864]{2,1,0:T(8,128)} %x_ref.1, f32[16,36864]{1,0:T(8,128)} %area_ref.1, bf16[1536,256]{1,0:T(8,128)(2,1)} %constant.37.clone.main_h, ...), custom_call_target="tpu_custom_call" | custom-call | tf_op jit(solution)/shard_map/stencil/pallas_call | solution.py:320
  57.0 0.0 all-gather.2.cloned.1.call-update
  57.0 0.0 all-reduce.3.cloned.1.call-start
  57.0 0.0 copy-done
  57.0 2.6 reshape.17
  59.6 9.8 %slice.3 = f32[16,48,48]{2,1,0:T(8,128)S(1)} slice(f32[16,192,192]{2,1,0:T(8,128)} %reshape.17), slice={[0:16:1], [1:192:4], [1:192:4]} | slice | bytes 294912 | tf_op jit(solution)/shard_map/slice | solution.py:358
  69.5 0.1 divide_sqrt_fusion
  69.6 0.1 reshape.18
  69.8 0.7 pad_bitcast_fusion.root_ref
  70.5 49.8 %all-gather.2.cloned.1.call-done.strips_ref = f32[96,2,32,128]{3,2,1,0:T(8,128)} async-done(((f32[12,2,32,128]{3,2,1,0:T(8,128)}), f32[96,2,32,128]{3,2,1,0:T(8,128)}) %all-gather.2.cloned.1.call-update) | async-done | bytes 3145744 | tf_op jit(solution)/shard_map/all_gather | solution.py:356
  120.3 9.6 %halo.1 = f32[24,384,128]{2,1,0:T(8,128)} custom-call(s32[1]{0:T(128)} %bitcast.first_ref, s32[96]{0:T(128)} %ids_ref.3, s32[1152]{0:T(1024)} %reshape.16.table_ref, f32[96,2,32,128]{3,2,1,0:T(8,128)} %all-gather.2.cloned.1.call-done.strips_ref, f32[24,384,128]{2,1,0:T(8,128)} %get-tuple-element.8.sums_ref, f32[24,16,128]{2,1,0:T(8,128)} %pad_bitcast_fusion.root_ref, ...), custom_call_target="tpu_custom_call" | custom-call | tf_op jit(solution)/shard_map/halo/pallas_call | solution.py:364
  129.9 59.8 %all_to_all.5.x_ref = f32[4,6,384,128]{3,2,1,0:T(8,128)} all-to-all(f32[4,6,384,128]{3,2,1,0:T(8,128)} %bitcast.4), channel_id=1, replica_groups=mesh['space'=8,'tm'=4] {'tm'}, dimensions={0} | all-to-all | bytes 9437184 | tf_op jit(solution)/shard_map/all_to_all | solution.py:386
  189.7 5.8 %gram.1 = f32[128,128]{1,0:T(8,128)} custom-call(f32[4,6,384,128]{3,2,1,0:T(8,128)} %all_to_all.5.x_ref), custom_call_target="tpu_custom_call" | custom-call | tf_op jit(solution)/shard_map/gram/pallas_call | solution.py:390
  195.5 0.0 all-reduce.3.cloned.1.call-update
  195.5 115.4 %all-reduce.3.cloned.1.call-done = f32[128,128]{1,0:T(8,128)} async-done(((f32[128,128]{1,0:T(8,128)}), f32[128,128]{1,0:T(8,128)}) %all-reduce.3.cloned.1.call-update) | async-done | bytes 65552 | tf_op jit(solution)/shard_map/psum | solution.py:400
  310.9 1.3 constant_dynamic-slice_fusion
  (1 shorter events, 0.0 us)
Async XLA Ops:
  6.5 113.8 %all-gather.2.cloned.1.call-start = ((), (), s32[]{:S(2)}) async-start(), calls=%async_computation.1 | async-start | bytes 3538944 | tf_op jit(solution)/shard_map/all_gather | solution.py:356
  8.1 48.9 %copy-start = (f32[16,36864]{1,0:T(8,128)S(1)}, f32[16,36864]{1,0:T(8,128)}, u32[]{:S(2)}) copy-start(f32[16,36864]{1,0:T(8,128)} %area_ref.1) | copy-start | bytes 7077892
  57.0 253.9 %all-reduce.3.cloned.1.call-start = ((), (), s32[]{:S(2)}) async-start(), calls=%async_computation.2 | async-start | bytes 131072 | tf_op jit(solution)/shard_map/psum | solution.py:400
Sparse Core Ops, SparseCore 0:
  57.1 63.1 all-gather.1
  195.7 115.2 all-reduce.2

commit v2 on v1

--- a/solution.py
+++ b/solution.py
@@ -19,6 +19,7 @@
 LANES = 128
 HALF = 64
 F32, BF16 = jnp.float32, jnp.bfloat16
+MESH = pl.DeviceIdType.MESH
 VMEM_LIMIT = 56 * 1024 * 1024
 
 
@@ -126,7 +127,36 @@
         matrix[chunk, LANES + HALF + index, slot * SIDE + SIDE - 1] = 1.0
     for lane in (SIDE, SIDE + 1, HALF + SIDE, HALF + SIDE + 1):
         matrix[0, lane, 0] = 1.0
-    return matrix.astype(ml_dtypes.bfloat16)
+    return matrix
+
+
+def pack(blocks, groups):
+    per_group = CHUNKS // groups
+    blocks = blocks.reshape((groups, per_group) + blocks.shape[1:])
+    spread = blocks[:, per_group - 1]
+    kept = []
+    for k in range(per_group - 1):
+        block = blocks[:, k, ..., : 2 * SIDE]
+        rest = spread[..., 32 * k : 32 * (k + 1)] if k < 3 else 0 * spread[..., :32]
+        join = np.concatenate if isinstance(blocks, np.ndarray) else jnp.concatenate
+        kept.append(join([block, rest], axis=-1))
+    stack = np.stack if isinstance(blocks, np.ndarray) else jnp.stack
+    return stack(kept, axis=1)
+
+
+def group_matrices(groups):
+    packed = pack(place_matrix(), groups)
+    count = packed.shape[1]
+    pick = np.zeros((groups, 2 * LANES, LANES))
+    place = np.zeros((groups, LANES, count * LANES))
+    for group in range(groups):
+        flat = packed[group].transpose(1, 0, 2).reshape(2 * LANES, count * LANES)
+        needed = np.nonzero(flat.any(axis=1))[0]
+        assert len(needed) <= LANES
+        for lane, source in enumerate(needed):
+            pick[group, source, lane] = 1.0
+            place[group, lane] = flat[source]
+    return pick.astype(ml_dtypes.bfloat16), place.astype(ml_dtypes.bfloat16)
 
 
 def split(x):
@@ -143,7 +173,7 @@
 
 
 def stencil_kernel(
-    tiles, snaps, slots, faces,
+    tiles, snaps, slots, faces, groups,
     first_ref, ids_ref, table_ref,
     x_ref, area_ref, main_h, main_l, up_h, up_l, down_h, down_l, order_ref,
     out_ref, send_ref,
@@ -197,6 +227,12 @@
             h, l = split(edges[block])
             matrix = order_ref[block * LANES : (block + 1) * LANES, :]
             sides = sides + dot(h, matrix) + dot(l, matrix)
+        for group in range(groups):
+            base = group * (CHUNKS // groups)
+            spread = out_ref[base + CHUNKS // groups - 1]
+            for k in range(3):
+                piece = pltpu.roll(spread, (2 * SIDE - 32 * k) % LANES, 1)
+                out_ref[base + k] = jnp.where(lane < 2 * SIDE, out_ref[base + k], piece)
         low_half = lane[:snaps] < HALF
         for t in range(tiles):
             part = slice(t * snaps, (t + 1) * snaps)
@@ -219,14 +255,13 @@
 
 
 def halo_kernel(
-    tiles, snaps, slots, faces, per_step,
+    tiles, snaps, slots, faces, groups,
     first_ref, ids_ref, table_ref,
-    strips_ref, sums_ref, root_ref, place_ref,
-    out_ref,
+    strips_ref, root_ref, pick_ref,
+    out_ref, weight_ref,
     high, low,
 ):
-    step = pl.program_id(0)
-    first = first_ref[0]
+    first, me = first_ref[0], first_ref[1]
     lane = lax.broadcasted_iota(jnp.int32, (snaps, LANES), 1)
 
     def near(slot, edge):
@@ -245,72 +280,152 @@
         value = strips_ref[far, 0]
         return jnp.where(lane == SIDE + col_end + HALF * row_end, value, 0.0)
 
-    @pl.when(step == 0)
-    def _():
-        for t in range(tiles):
-            slot = first + t
-            part = pl.ds(t * snaps, snaps)
-            for pair in range(2):
-                strips = []
-                for k in range(2):
-                    far, far_edge, _ = near(slot, 2 * pair + k)
-                    value = strips_ref[far, lax.div(far_edge, 2)]
-                    rolled = pltpu.roll(value, HALF, 1)
-                    same = (jnp.zeros((snaps, LANES), jnp.int32) + lax.rem(far_edge, 2)) == k
-                    strips.append(jnp.where(same, value, rolled))
-                both = jnp.where(lane < HALF, strips[0], strips[1])
-                both = jnp.where(lane % HALF < SIDE, both, 0.0)
-                if pair == 0:
-                    both = both + CORNER * (corner(slot, 0) + corner(slot, 2))
-                h, l = split(both)
-                high[part, pair * LANES : (pair + 1) * LANES] = h
-                low[part, pair * LANES : (pair + 1) * LANES] = l
-
-    for chunk in range(per_step):
-        added = dot(high[...], place_ref[chunk]) + dot(low[...], place_ref[chunk])
-        for t in range(tiles):
-            part = slice(t * snaps, (t + 1) * snaps)
-            face = lax.rem(ids_ref[first + t], faces)
-            out_ref[chunk, part, :] = (sums_ref[chunk, part, :] + added[part, :]) * root_ref[
-                chunk, pl.ds(face, 1), :
-            ]
-
-
-def gram_kernel(tiles, snaps, groups, scale, x_ref, out_ref, main, cross):
-    step = pl.program_id(0)
-
-    @pl.when(step == 0)
-    def _():
-        main[...] = jnp.zeros_like(main)
-        cross[...] = jnp.zeros_like(cross)
-
+    for t in range(tiles):
+        slot = first + t
+        part = pl.ds(t * snaps, snaps)
+        for pair in range(2):
+            strips = []
+            for k in range(2):
+                far, far_edge, _ = near(slot, 2 * pair + k)
+                value = strips_ref[far, lax.div(far_edge, 2)]
+                rolled = pltpu.roll(value, HALF, 1)
+                same = (jnp.zeros((snaps, LANES), jnp.int32) + lax.rem(far_edge, 2)) == k
+                strips.append(jnp.where(same, value, rolled))
+            both = jnp.where(lane < HALF, strips[0], strips[1])
+            both = jnp.where(lane % HALF < SIDE, both, 0.0)
+            if pair == 0:
+                both = both + CORNER * (corner(slot, 0) + corner(slot, 2))
+            h, l = split(both)
+            high[part, pair * LANES : (pair + 1) * LANES] = h
+            low[part, pair * LANES : (pair + 1) * LANES] = l
+
+    for group in range(groups):
+        out_ref[group] = dot(high[...], pick_ref[group]) + dot(low[...], pick_ref[group])
+    for t in range(tiles):
+        face = lax.rem(ids_ref[first + t], faces)
+        for block in range(weight_ref.shape[0]):
+            weight_ref[block, t : t + 1, :] = root_ref[me, block, pl.ds(face, 1), :]
+
+
+def exchange_kernel(groups, src_ref, dst_ref, local_sem, send_sem, recv_sem):
+    me = lax.axis_index("tm")
+    count = dst_ref.shape[1]
+    barrier = pltpu.get_barrier_semaphore()
+    for k in range(1, groups):
+        pl.semaphore_signal(
+            barrier, inc=1, device_id={"tm": lax.rem(me + k, groups)}, device_id_type=MESH
+        )
+    pl.semaphore_wait(barrier, groups - 1)
+    copies = []
+    for k in sorted(range(1, groups), key=lambda k: abs(k - groups // 2)):
+        to = lax.rem(me + k, groups)
+        copy = pltpu.make_async_remote_copy(
+            src_ref=src_ref.at[to, pl.ds(0, count)],
+            dst_ref=dst_ref.at[me],
+            send_sem=send_sem.at[k],
+            recv_sem=recv_sem.at[k],
+            device_id={"tm": to},
+            device_id_type=MESH,
+        )
+        copy.start()
+        copies.append(copy)
+    own = pltpu.make_async_copy(src_ref.at[me, pl.ds(0, count)], dst_ref.at[me], local_sem)
+    own.start()
+    own.wait()
+    for copy in copies:
+        copy.wait()
+
+
+def gram_kernel(
+    tiles, snaps, groups, spaces, scale,
+    shared_ref, halo_ref, weight_ref, place_ref,
+    out_ref,
+    strips, high, low, part, from_tm, from_space,
+    strip_sems, tm_sems, space_sems,
+):
+    me = lax.axis_index("tm")
+    here = lax.axis_index("space")
+    barrier = pltpu.get_barrier_semaphore()
+    for k in range(1, groups):
+        pl.semaphore_signal(
+            barrier, inc=1, device_id={"tm": lax.rem(me + k, groups)}, device_id_type=MESH
+        )
+    for k in range(1, spaces):
+        pl.semaphore_signal(
+            barrier, inc=1, device_id={"space": lax.rem(here + k, spaces)}, device_id_type=MESH
+        )
+    pl.semaphore_wait(barrier, groups + spaces - 2)
+
+    def send(src, dst, sems, k, device):
+        copy = pltpu.make_async_remote_copy(
+            src_ref=src,
+            dst_ref=dst,
+            send_sem=sems.at[0, k],
+            recv_sem=sems.at[1, k],
+            device_id=device,
+            device_id_type=MESH,
+        )
+        copy.start()
+        return copy
+
+    copies = []
+    for k in range(1, groups):
+        to = lax.rem(me + k, groups)
+        copies.append(send(halo_ref.at[to], strips.at[k], strip_sems, k, {"tm": to}))
+    strips[0] = halo_ref[me]
+    for copy in copies:
+        copy.wait()
+
+    blocks = shared_ref.shape[1]
+    place = place_ref[me]
+    for group in range(groups):
+        h, l = split(strips[lax.rem(me - group + groups, groups)])
+        rows = slice(group * snaps, (group + 1) * snaps)
+        for block in range(blocks):
+            matrix = place[:, block * LANES : (block + 1) * LANES]
+            added = dot(h, matrix) + dot(l, matrix) + shared_ref[group, block]
+            for t in range(tiles):
+                x = added[t * snaps : (t + 1) * snaps] * weight_ref[block, t : t + 1, :]
+                xh, xl = split(x)
+                at = (block * tiles + t) * LANES
+                high[rows, at : at + LANES] = xh
+                low[rows, at : at + LANES] = xl
     dims = (((1,), (1,)), ((), ()))
-    count = groups * snaps
-    highs, lows = [], []
-    for t in range(tiles):
-        x = x_ref[:, 0, t * snaps : (t + 1) * snaps, :].reshape(count, LANES)
-        h, l = split(x)
-        highs.append(h)
-        lows.append(l)
-    h = jnp.concatenate(highs, axis=1)
-    l = jnp.concatenate(lows, axis=1)
-    main[...] += lax.dot_general(h, h, dims, preferred_element_type=F32)
-    cross[...] += lax.dot_general(h, l, dims, preferred_element_type=F32)
-
-    @pl.when(step == pl.num_programs(0) - 1)
-    def _():
-        out_ref[...] = (main[...] + cross[...] + cross[...].T) * scale
+    main = lax.dot_general(high[...], high[...], dims, preferred_element_type=F32)
+    cross = lax.dot_general(high[...], low[...], dims, preferred_element_type=F32)
+    part[...] = ((main + cross + cross.T) * scale).reshape(part.shape)
+
+    copies = []
+    for k in range(1, groups):
+        to = lax.rem(me + k, groups)
+        copies.append(send(part.at[to], from_tm.at[k], tm_sems, k, {"tm": to}))
+    for copy in copies:
+        copy.wait()
+    total = part[me]
+    for k in range(1, groups):
+        total = total + from_tm[k]
+    from_space[0] = total
+    copies = []
+    for k in range(1, spaces):
+        to = lax.rem(here + k, spaces)
+        copies.append(send(from_space.at[0], from_space.at[k], space_sems, k, {"space": to}))
+    for copy in copies:
+        copy.wait()
+    total = from_space[here]
+    for source in range(1, spaces):
+        total = total + from_space[lax.rem(here - source + spaces, spaces)]
+    out_ref[...] = total
 
 
 def full(shape):
     return pl.BlockSpec(shape, lambda c, *_: (0,) * len(shape))
 
 
-def body(groups, pw_field, cell_area, tile_ids, edge_table):
+def body(groups, spaces, pw_field, cell_area, tile_ids, edge_table):
     tiles, snaps, cells = pw_field.shape
     slots, faces = tile_ids.shape[0], cell_area.shape[0]
     rows = tiles * snaps
-    first = (lax.axis_index("space") * tiles).astype(jnp.int32).reshape(1)
+    first = jnp.stack([lax.axis_index("space") * tiles, lax.axis_index("tm")]).astype(jnp.int32)
     table = edge_table.reshape(-1)
     main_h, main_l = split_const(chunk_matrix())
     upper, lower = rim_matrices()
@@ -318,7 +433,7 @@
     down_h, down_l = split_const(lower)
 
     sums, send = pl.pallas_call(
-        functools.partial(stencil_kernel, tiles, snaps, slots, faces),
+        functools.partial(stencil_kernel, tiles, snaps, slots, faces, groups),
         grid_spec=pltpu.PrefetchScalarGridSpec(
             num_scalar_prefetch=3,
             grid=(CHUNKS,),
@@ -358,52 +473,80 @@
     sampled = cell_area.reshape(faces, TILE, TILE)[:, 1::STRIDE, 1::STRIDE]
     root = jnp.sqrt(1.0 / sampled).reshape(faces, CHUNKS, 2 * SIDE)
     root = jnp.pad(root, ((0, 0), (0, 0), (0, LANES - 2 * SIDE)))
-    root = jnp.transpose(root, (1, 0, 2))
-
-    per_step = CHUNKS // groups
-    scaled = pl.pallas_call(
-        functools.partial(halo_kernel, tiles, snaps, slots, faces, per_step),
+    root = pack(jnp.transpose(root, (1, 0, 2)), groups)
+    pick, place = group_matrices(groups)
+    blocks = root.shape[1]
+
+    shared = pl.pallas_call(
+        functools.partial(exchange_kernel, groups),
+        in_specs=[pl.BlockSpec(memory_space=pl.ANY)],
+        out_specs=pl.BlockSpec(memory_space=pl.ANY),
+        scratch_shapes=[
+            pltpu.SemaphoreType.DMA,
+            pltpu.SemaphoreType.DMA((groups,)),
+            pltpu.SemaphoreType.DMA((groups,)),
+        ],
+        out_shape=jax.ShapeDtypeStruct((groups, blocks, rows, LANES), F32),
+        compiler_params=pltpu.CompilerParams(
+            collective_id=0, has_side_effects=True, vmem_limit_bytes=VMEM_LIMIT
+        ),
+        cost_estimate=pl.CostEstimate(
+            flops=0, bytes_accessed=32 * CHUNKS * rows * LANES, transcendentals=0
+        ),
+        name="exchange",
+    )(sums.reshape(groups, CHUNKS // groups, rows, LANES))
+
+    halos, weights = pl.pallas_call(
+        functools.partial(halo_kernel, tiles, snaps, slots, faces, groups),
         grid_spec=pltpu.PrefetchScalarGridSpec(
             num_scalar_prefetch=3,
-            grid=(groups,),
+            grid=(1,),
             in_specs=[
                 full((slots, 2, snaps, LANES)),
-                pl.BlockSpec((per_step, rows, LANES), lambda c, *_: (c, 0, 0)),
-                pl.BlockSpec((per_step, faces, LANES), lambda c, *_: (c, 0, 0)),
-                pl.BlockSpec((per_step, 2 * LANES, LANES), lambda c, *_: (c, 0, 0)),
+                full((groups, blocks, faces, LANES)),
+                full((groups, 2 * LANES, LANES)),
             ],
-            out_specs=pl.BlockSpec((per_step, rows, LANES), lambda c, *_: (c, 0, 0)),
+            out_specs=[full((groups, rows, LANES)), full((blocks, tiles, LANES))],
             scratch_shapes=[
                 pltpu.VMEM((rows, 2 * LANES), BF16),
                 pltpu.VMEM((rows, 2 * LANES), BF16),
             ],
         ),
-        out_shape=jax.ShapeDtypeStruct((CHUNKS, rows, LANES), F32),
+        out_shape=[
+            jax.ShapeDtypeStruct((groups, rows, LANES), F32),
+            jax.ShapeDtypeStruct((blocks, tiles, LANES), F32),
+        ],
         compiler_params=pltpu.CompilerParams(vmem_limit_bytes=VMEM_LIMIT),
         name="halo",
-    )(first, tile_ids, table, strips, sums, root, place_matrix())
-
-    shared = lax.all_to_all(
-        scaled.reshape(groups, per_step, rows, LANES), "tm", split_axis=0, concat_axis=0
-    )
+    )(first, tile_ids, table, strips, root, pick)
+
     count = groups * snaps
-    partial_gram = pl.pallas_call(
-        functools.partial(gram_kernel, tiles, snaps, groups, 1.0 / (slots * SIDE * SIDE)),
-        grid=(per_step,),
-        in_specs=[pl.BlockSpec((groups, 1, rows, LANES), lambda c: (0, c, 0, 0))],
-        out_specs=pl.BlockSpec((count, count), lambda c: (0, 0)),
-        scratch_shapes=[pltpu.VMEM((count, count), F32), pltpu.VMEM((count, count), F32)],
-        out_shape=jax.ShapeDtypeStruct((count, count), F32),
-        compiler_params=pltpu.CompilerParams(vmem_limit_bytes=VMEM_LIMIT),
+    return pl.pallas_call(
+        functools.partial(gram_kernel, tiles, snaps, groups, spaces, 1.0 / (slots * SIDE * SIDE)),
+        in_specs=[pl.BlockSpec(memory_space=pltpu.VMEM)] * 4,
+        out_specs=pl.BlockSpec(memory_space=pltpu.VMEM),
+        scratch_shapes=[
+            pltpu.VMEM((groups, rows, LANES), F32),
+            pltpu.VMEM((count, tiles * blocks * LANES), BF16),
+            pltpu.VMEM((count, tiles * blocks * LANES), BF16),
+            pltpu.VMEM((groups, snaps, count), F32),
+            pltpu.VMEM((groups, snaps, count), F32),
+            pltpu.VMEM((spaces, snaps, count), F32),
+            pltpu.SemaphoreType.DMA((2, groups)),
+            pltpu.SemaphoreType.DMA((2, groups)),
+            pltpu.SemaphoreType.DMA((2, spaces)),
+        ],
+        out_shape=jax.ShapeDtypeStruct((snaps, count), F32),
+        compiler_params=pltpu.CompilerParams(
+            collective_id=1, has_side_effects=True, vmem_limit_bytes=VMEM_LIMIT
+        ),
         name="gram",
-    )(shared)
-    total = lax.psum(partial_gram, ("space", "tm"))
-    return lax.dynamic_slice_in_dim(total, lax.axis_index("tm") * snaps, snaps, 0)
+    )(shared, halos, weights, place)
 
 
 def solution(mesh):
     placed = (P("space", "tm", None), P(), P(), P())
     return jax.shard_map(
-        functools.partial(body, mesh.shape["tm"]),
+        functools.partial(body, mesh.shape["tm"], mesh.shape["space"]),
         mesh=mesh, in_specs=placed, out_specs=P("tm", None), check_vma=False,
     )

time: 321 us -> 159 us (0.50)
  waiting for transfers between devices: 165 us -> 3.41 us
  Pallas kernels: 64.3 us -> 125 us
  blocking collectives: 59.8 us -> 0 us
    psum x1 -> x0, waiting for transfers between devices: 115 us -> none  [body(): total = lax.psum(partial_gram, ('space', 'tm'))]
    pallas_call x1 -> x2, Pallas kernels: 5.81 us -> 71.1 us  [the longest x1 46.6 us: body(): pl.pallas_call(functools.partial(exchange_kernel, groups), in_specs=[pl.B...]
    all_to_all x1 -> x0, blocking collectives: 59.8 us -> none  [body(): lax.all_to_all(scaled.reshape(groups, per_step, rows, LANES), 'tm', split...]
    all_gather x1, waiting for transfers between devices: 49.8 us -> 3.4 us  [body(): strips = lax.all_gather(send, 'space', axis=0, tiled=True)]
    pallas_call x1, Pallas kernels: 9.63 us -> 4.76 us  [body(): pl.pallas_call(functools.partial(halo_kernel, tiles, snaps, slots, faces,...]
  transfers between devices with their start and end apart: 2 -> 1, of which waited for: 2 -> 1; matrix products, arithmetic and copies ran while one was open for 4% -> 8% of each run, Pallas kernels for 0% -> 29%
where the time goes in v2:
time: 159 us; the launch traced here: 158 us
  Pallas kernels  125 us (79%)
  local copies, waits for them, and re-layouts  15.5 us (10%)
  between operations  13.5 us (8%)
  waiting for transfers between devices  3.41 us (2%)
    pallas_call x1, Pallas kernels, body(): pl.pallas_call(functools.partial(stencil_kernel, tiles, snaps, slots, fac...  48.9 us
    pallas_call x1, Pallas kernels, body(): pl.pallas_call(functools.partial(exchange_kernel, groups), in_specs=[pl.B...  46.6 us
    pallas_call x1, Pallas kernels, body(): pl.pallas_call(functools.partial(gram_kernel, tiles, snaps, groups, space...  24.4 us
    slice x1, local copies, waits for them, and re-layouts, body(): sampled = cell_area.reshape(faces, TILE, TILE)[:, 1::STRIDE, 1::STRIDE]  9.82 us
    pallas_call x1, Pallas kernels, body(): pl.pallas_call(functools.partial(halo_kernel, tiles, snaps, slots, faces,...  4.76 us
    all_gather x1, waiting for transfers between devices, body(): strips = lax.all_gather(send, 'space', axis=0, tiled=True)  3.4 us
  transfers between devices with their start and end apart: 1, of which 1 were waited for; matrix products, arithmetic and copies ran while one was open for 8% of the time, Pallas kernels for 29%

profile of v2, /device:TPU:0, one launch (start us, length us, event | category | flops | bytes accessed | tf_op | source)
XLA Modules:
  0.0 158.3 jit_solution(5183112482345055382)
XLA Ops:
  6.5 0.0 all-gather.2.cloned.1.call-start
  6.5 0.8 copy.33
  7.3 0.7 reshape.15.table_ref
  8.1 0.6 pad_add_fusion.first_ref
  8.7 0.0 copy-start
  8.7 48.9 %stencil.1 = (f32[24,384,128]{2,1,0:T(8,128)}, f32[12,2,32,128]{3,2,1,0:T(8,128)}) custom-call(s32[2]{0:T(128)} %pad_add_fusion.first_ref, s32[96]{0:T(128)} %ids_ref.3, s32[1152]{0:T(1024)} %reshape.15.table_ref, f32[12,32,36864]{2,1,0:T(8,128)} %x_ref.1, f32[16,36864]{1,0:T(8,128)} %area_ref.1, bf16[1536,256]{1,0:T(8,128)(2,1)} %constant.35.clone.main_h, ...), custom_call_target="tpu_custom_call" | custom-call | tf_op jit(solution)/shard_map/stencil/pallas_call | solution.py:435
  57.6 0.0 all-gather.2.cloned.1.call-update
  57.6 0.0 copy-done
  57.6 2.6 %reshape.17 = f32[16,192,192]{2,1,0:T(8,128)} reshape(f32[16,36864]{1,0:T(8,128)S(1)} %copy-done) | data formatting | bytes 4718592 | tf_op jit(solution)/shard_map/reshape | solution.py:473
  60.2 9.8 %slice.32 = f32[16,48,48]{2,1,0:T(8,128)S(1)} slice(f32[16,192,192]{2,1,0:T(8,128)} %reshape.17), slice={[0:16:1], [1:192:4], [1:192:4]} | slice | bytes 294912 | tf_op jit(solution)/shard_map/slice | solution.py:473
  70.1 0.1 divide_sqrt_fusion
  70.2 0.1 reshape.18
  70.4 46.6 %exchange.1.shared_ref = f32[4,5,384,128]{3,2,1,0:T(8,128)} custom-call(f32[4,6,384,128]{3,2,1,0:T(8,128)} %bitcast.50), custom_call_target="tpu_custom_call" | custom-call | bytes 37748736 | tf_op jit(solution)/shard_map/exchange/pallas_call | solution.py:480
  117.0 0.1 broadcast_multiply_fusion
  117.1 0.1 fusion
  117.2 0.1 fusion.1
  117.3 0.1 fusion.2
  117.4 0.1 fusion.3
  117.5 0.1 fusion.4.root_ref
  117.5 0.0 copy-start.1
  117.5 3.4 %all-gather.2.cloned.1.call-done.strips_ref = f32[96,2,32,128]{3,2,1,0:T(8,128)} async-done(((f32[12,2,32,128]{3,2,1,0:T(8,128)}), f32[96,2,32,128]{3,2,1,0:T(8,128)}) %all-gather.2.cloned.1.call-update) | async-done | bytes 3145744 | tf_op jit(solution)/shard_map/all_gather | solution.py:471
  120.9 0.0 copy-done.1
  120.9 4.8 %halo.1 = (f32[4,384,128]{2,1,0:T(8,128)}, f32[5,12,128]{2,1,0:T(8,128)}) custom-call(s32[2]{0:T(128)} %pad_add_fusion.first_ref, s32[96]{0:T(128)} %ids_ref.3, s32[1152]{0:T(1024)} %reshape.15.table_ref, f32[96,2,32,128]{3,2,1,0:T(8,128)} %all-gather.2.cloned.1.call-done.strips_ref, f32[4,5,16,128]{3,2,1,0:T(8,128)} %copy-done.1, ...), custom_call_target="tpu_custom_call" | custom-call | tf_op jit(solution)/shard_map/halo/pallas_call | solution.py:499
  125.7 24.4 %gram.1 = f32[32,128]{1,0:T(8,128)} custom-call(f32[4,5,384,128]{3,2,1,0:T(8,128)} %exchange.1.shared_ref, f32[4,384,128]{2,1,0:T(8,128)} %get-tuple-element.11.halo_ref, f32[5,12,128]{2,1,0:T(8,128)} %get-tuple-element.12.weight_ref, bf16[4,128,640]{2,1,0:T(8,128)(2,1)} %constant.43.clone.place_ref), custom_call_target="tpu_custom_call" | custom-call | tf_op jit(solution)/shard_map/gram/pallas_call | solution.py:524
  150.2 1.3 copy.52
  (4 shorter events, 0.1 us)
Async XLA Ops:
  6.5 114.4 %all-gather.2.cloned.1.call-start = ((), (), s32[]{:S(2)}) async-start(), calls=%async_computation | async-start | bytes 3538944 | tf_op jit(solution)/shard_map/all_gather | solution.py:471
  8.7 48.9 %copy-start = (f32[16,36864]{1,0:T(8,128)S(1)}, f32[16,36864]{1,0:T(8,128)}, u32[]{:S(2)}) copy-start(f32[16,36864]{1,0:T(8,128)} %area_ref.1) | copy-start | bytes 7077892
  117.5 3.4 %copy-start.1 = (f32[4,5,16,128]{3,2,1,0:T(8,128)}, f32[4,5,16,128]{3,2,1,0:T(8,128)S(1)}, u32[]{:S(2)}) copy-start(f32[4,5,16,128]{3,2,1,0:T(8,128)S(1)} %fusion.4.root_ref) | copy-start | bytes 491524
Sparse Core Ops, SparseCore 0:
  57.8 63.1 all-gather.1

commit v3 on v2

--- a/solution.py
+++ b/solution.py
@@ -182,12 +182,16 @@
     step = pl.program_id(0)
     first = first_ref[0]
     rows = tiles * snaps
-    for t in range(tiles):
-        face = lax.rem(ids_ref[first + t], faces)
-        part = pl.ds(t * snaps, snaps)
-        h, l = split(x_ref[t] * area_ref[pl.ds(face, 1), :])
-        high[part, :] = h
-        low[part, :] = l
+    result = jnp.zeros((rows, 2 * LANES), F32)
+    for half in range(2):
+        cells = slice(half * RIM, (half + 1) * RIM)
+        for t in range(tiles):
+            face = lax.rem(ids_ref[first + t], faces)
+            part = slice(t * snaps, (t + 1) * snaps)
+            h, l = split(x_ref[t, :, cells] * area_ref[pl.ds(face, 1), cells])
+            high[part, cells] = h
+            low[part, cells] = l
+        result = result + dot3(high[:, cells], low[:, cells], main_h[cells, :], main_l[cells, :])
     lane = lax.broadcasted_iota(jnp.int32, (rows, LANES), 1)
     from_before = (lane < SIDE) | ((lane >= 2 * SIDE) & (lane % 2 == 0))
     is_edge = (lane >= 2 * SIDE) & (lane < 2 * SIDE + 16)
@@ -203,7 +207,6 @@
         edges[...] = jnp.zeros_like(edges)
         rims[...] = dot3(high[:, :RIM], low[:, :RIM], up_h[...], up_l[...])
 
-    result = dot3(high[...], low[...], main_h[...], main_l[...])
     own, other = result[:, :LANES], result[:, LANES:]
 
     @pl.when(step > 0)

time: 159 us -> 156 us (0.981)
  Pallas kernels: 125 us -> 122 us
    pallas_call x1, Pallas kernels: 48.9 us -> 45.8 us  [body(): pl.pallas_call(functools.partial(stencil_kernel, tiles, snaps, slots, fac...]
  transfers between devices with their start and end apart: 1 -> 1, of which waited for: 1 -> 1; matrix products, arithmetic and copies ran while one was open for 8% -> 8% of each run, Pallas kernels for 29% -> 30%
where the time goes in v3:
time: 156 us; the launch traced here: 155 us
  Pallas kernels  122 us (78%)
  local copies, waits for them, and re-layouts  15.5 us (10%)
  between operations  13.5 us (9%)
  waiting for transfers between devices  3.41 us (2%)
    pallas_call x1, Pallas kernels, body(): pl.pallas_call(functools.partial(exchange_kernel, groups), in_specs=[pl.B...  46.6 us
    pallas_call x1, Pallas kernels, body(): pl.pallas_call(functools.partial(stencil_kernel, tiles, snaps, slots, fac...  45.8 us
    pallas_call x1, Pallas kernels, body(): pl.pallas_call(functools.partial(gram_kernel, tiles, snaps, groups, space...  24.4 us
    slice x1, local copies, waits for them, and re-layouts, body(): sampled = cell_area.reshape(faces, TILE, TILE)[:, 1::STRIDE, 1::STRIDE]  9.82 us
    pallas_call x1, Pallas kernels, body(): pl.pallas_call(functools.partial(halo_kernel, tiles, snaps, slots, faces,...  4.76 us
    all_gather x1, waiting for transfers between devices, body(): strips = lax.all_gather(send, 'space', axis=0, tiled=True)  3.4 us
  transfers between devices with their start and end apart: 1, of which 1 were waited for; matrix products, arithmetic and copies ran while one was open for 8% of the time, Pallas kernels for 30%

profile of v3, /device:TPU:0, one launch (start us, length us, event | category | flops | bytes accessed | tf_op | source)
XLA Modules:
  0.0 155.3 jit_solution(678494748574217977)
XLA Ops:
  6.5 0.0 all-gather.2.cloned.1.call-start
  6.5 0.8 copy.33
  7.3 0.7 reshape.15.table_ref
  8.1 0.6 pad_add_fusion.first_ref
  8.7 0.0 copy-start
  8.7 45.8 %stencil.1 = (f32[24,384,128]{2,1,0:T(8,128)}, f32[12,2,32,128]{3,2,1,0:T(8,128)}) custom-call(s32[2]{0:T(128)} %pad_add_fusion.first_ref, s32[96]{0:T(128)} %ids_ref.3, s32[1152]{0:T(1024)} %reshape.15.table_ref, f32[12,32,36864]{2,1,0:T(8,128)} %x_ref.1, f32[16,36864]{1,0:T(8,128)} %area_ref.1, bf16[1536,256]{1,0:T(8,128)(2,1)} %constant.35.clone.main_h, ...), custom_call_target="tpu_custom_call" | custom-call | tf_op jit(solution)/shard_map/stencil/pallas_call | solution.py:438
  54.5 0.0 all-gather.2.cloned.1.call-update
  54.6 0.0 copy-done
  54.6 2.6 %reshape.17 = f32[16,192,192]{2,1,0:T(8,128)} reshape(f32[16,36864]{1,0:T(8,128)S(1)} %copy-done) | data formatting | bytes 4718592 | tf_op jit(solution)/shard_map/reshape | solution.py:476
  57.2 9.8 %slice.32 = f32[16,48,48]{2,1,0:T(8,128)S(1)} slice(f32[16,192,192]{2,1,0:T(8,128)} %reshape.17), slice={[0:16:1], [1:192:4], [1:192:4]} | slice | bytes 294912 | tf_op jit(solution)/shard_map/slice | solution.py:476
  67.0 0.1 divide_sqrt_fusion
  67.1 0.1 reshape.18
  67.3 46.6 %exchange.1.shared_ref = f32[4,5,384,128]{3,2,1,0:T(8,128)} custom-call(f32[4,6,384,128]{3,2,1,0:T(8,128)} %bitcast.50), custom_call_target="tpu_custom_call" | custom-call | bytes 37748736 | tf_op jit(solution)/shard_map/exchange/pallas_call | solution.py:483
  114.0 0.1 broadcast_multiply_fusion
  114.1 0.1 fusion
  114.1 0.1 fusion.1
  114.2 0.1 fusion.2
  114.3 0.1 fusion.3
  114.4 0.1 fusion.4.root_ref
  114.5 0.0 copy-start.1
  114.5 3.4 %all-gather.2.cloned.1.call-done.strips_ref = f32[96,2,32,128]{3,2,1,0:T(8,128)} async-done(((f32[12,2,32,128]{3,2,1,0:T(8,128)}), f32[96,2,32,128]{3,2,1,0:T(8,128)}) %all-gather.2.cloned.1.call-update) | async-done | bytes 3145744 | tf_op jit(solution)/shard_map/all_gather | solution.py:474
  117.9 0.0 copy-done.1
  117.9 4.8 %halo.1 = (f32[4,384,128]{2,1,0:T(8,128)}, f32[5,12,128]{2,1,0:T(8,128)}) custom-call(s32[2]{0:T(128)} %pad_add_fusion.first_ref, s32[96]{0:T(128)} %ids_ref.3, s32[1152]{0:T(1024)} %reshape.15.table_ref, f32[96,2,32,128]{3,2,1,0:T(8,128)} %all-gather.2.cloned.1.call-done.strips_ref, f32[4,5,16,128]{3,2,1,0:T(8,128)} %copy-done.1, ...), custom_call_target="tpu_custom_call" | custom-call | tf_op jit(solution)/shard_map/halo/pallas_call | solution.py:502
  122.6 24.4 %gram.1 = f32[32,128]{1,0:T(8,128)} custom-call(f32[4,5,384,128]{3,2,1,0:T(8,128)} %exchange.1.shared_ref, f32[4,384,128]{2,1,0:T(8,128)} %get-tuple-element.11.halo_ref, f32[5,12,128]{2,1,0:T(8,128)} %get-tuple-element.12.weight_ref, bf16[4,128,640]{2,1,0:T(8,128)(2,1)} %constant.43.clone.place_ref), custom_call_target="tpu_custom_call" | custom-call | tf_op jit(solution)/shard_map/gram/pallas_call | solution.py:527
  147.1 1.3 copy.52
  (4 shorter events, 0.1 us)
Async XLA Ops:
  6.5 111.3 %all-gather.2.cloned.1.call-start = ((), (), s32[]{:S(2)}) async-start(), calls=%async_computation | async-start | bytes 3538944 | tf_op jit(solution)/shard_map/all_gather | solution.py:474
  8.7 45.8 %copy-start = (f32[16,36864]{1,0:T(8,128)S(1)}, f32[16,36864]{1,0:T(8,128)}, u32[]{:S(2)}) copy-start(f32[16,36864]{1,0:T(8,128)} %area_ref.1) | copy-start | bytes 7077892
  114.5 3.4 %copy-start.1 = (f32[4,5,16,128]{3,2,1,0:T(8,128)}, f32[4,5,16,128]{3,2,1,0:T(8,128)S(1)}, u32[]{:S(2)}) copy-start(f32[4,5,16,128]{3,2,1,0:T(8,128)S(1)} %fusion.4.root_ref) | copy-start | bytes 491524
Sparse Core Ops, SparseCore 0:
  54.7 63.1 all-gather.1
